TPU v7x, 512 devices: a whole 4x4x16 slice. The times are simulated.
512 devices in a mesh: dom: 64 (over x, z), orb: 8 (over y, core).
Axes of the slice: x: 4, y: 4, z: 16, core: 2. Of those that a mesh axis runs over, the one named last changes fastest.
Arguments:
- orbitals: bfloat16 [3072, 64, 512], P('dom', 'orb'), may hold values from -6 to 6
- adjoint_source: bfloat16 [3072, 64, 512], P('dom', 'orb'), may hold values from -6 to 6
- eigenvalues: float32 [64], P('orb'), may hold values from -1 to -0.25
- cell_scale: float32 [3072], P('dom'), may hold values from 0.4 to 1.6
- base_potential: float32 [3072, 512], P('dom'), may hold values from 0.5 to 1.5
- stiffness: bfloat16 [512, 512], replicated, may hold values from -1.5 to 1.5, as said below
- face_perm: int32 [3072, 64], P('dom'), may hold values from 0 to 63, each once within a row
- restrict: bfloat16 [512, 64], replicated, may hold values from -0.25 to 0.25
- prolong: bfloat16 [64, 512], replicated, may hold values from -0.75 to 0.75
- owner: int32 [3072, 1], P('dom'), may hold values from 0 to 63; in each aligned block of 48 rows (0 to 47, 48 to 95, ...) at most 2 rows name the same one
- pot_slot: int32 [3072], P('dom'), may hold values from 0 to 63
- potential: float32 [4096, 64], P('dom'), may hold values from -6 to 6
Outputs:
- adjoint: bfloat16 [3072, 64, 512], P('dom', 'orb')
- updated: float32 [4096, 64], P('dom')
- applied: bfloat16 [3072, 64, 512], P('dom', 'orb')
Inputs may be any that keep to these rules, and one draw needn't show every extreme that they name: In the rows of one device no owner is named by more than 2 cells. `face_perm`: each row is a permutation. `stiffness`: symmetric.
All inputs are finite; a program needn't handle non-finite values.
Results may differ from a plain program's by a relative error of at most 0.0027.
Values sent between devices are 32-bit elements; how exact they have to be, the bound alone decides.
No kernel may reach another device: no remote copies, remote signals or barrier semaphores. Data moves between devices by JAX's collectives and lax.ppermute only.
A program may use at most 64 MiB of HBM per device.

v0:
```python
import jax
import jax.numpy as jnp
from jax import lax
from jax.sharding import PartitionSpec as P

ITERS = 4
relax = 0.25
step_rate = 0.1


def padded_2(block, sides, width):
    for axis, dim in sides:
        count = lax.axis_size(axis)
        forward = [(i, i + 1) for i in range(count - 1)]
        backward = [(target, source) for source, target in forward]
        low = lax.ppermute(
            lax.slice_in_dim(block, block.shape[dim] - width, None, axis=dim), axis, forward
        )
        high = lax.ppermute(lax.slice_in_dim(block, 0, width, axis=dim), axis, backward)
        block = jnp.concatenate([low, block, high], axis=dim)
    return block


def local(
    orbitals,
    adjoint_source,
    eigenvalues,
    cell_scale,
    base_potential,
    stiffness,
    face_perm,
    restrict,
    prolong,
    owner,
    pot_slot,
    potential,
):
    nodes = stiffness.shape[0]
    faces = face_perm.shape[1]
    pot_rows = potential.shape[0]
    n_domains = lax.axis_size("dom")
    cell_count = owner.shape[0]
    capacity = 2 * ((cell_count + n_domains - 1) // n_domains)
    onehot = (face_perm[:, :, None] == jnp.arange(faces, dtype=jnp.int32)[None, None, :]).astype(
        jnp.float32
    )

    def assemble_local(partial_sum):
        left_face = partial_sum[:, :, :faces]
        right_face = partial_sum[:, :, nodes - faces :]
        sent_right = jnp.einsum("ckj,cok->coj", onehot, right_face, precision=lax.Precision.HIGHEST)
        boundary = jnp.stack([left_face[0], sent_right[-1]], 0)
        padded = padded_2(boundary, (("dom", 0),), 1)
        left_next = jnp.concatenate([left_face[1:], padded[3][None]], 0)
        add_right = jnp.einsum("ckj,coj->cok", onehot, left_next, precision=lax.Precision.HIGHEST)
        add_left = jnp.concatenate([padded[0][None], sent_right[:-1]], 0)
        return jnp.concatenate(
            [
                left_face + add_left,
                partial_sum[:, :, faces : nodes - faces],
                right_face + add_right,
            ],
            2,
        )

    def operator(values_bf, values_full, shift):
        kinetic = jnp.dot(
            values_bf.reshape(-1, nodes), stiffness, preferred_element_type=jnp.float32
        ).reshape(values_full.shape)
        return assemble_local(cell_scale[:, None, None] * kinetic + shift * values_full)

    source = adjoint_source.astype(jnp.float32)
    shift = base_potential[:, None, :] - eigenvalues[None, :, None]
    iterate = relax * source
    for step_index in range(ITERS):
        image = operator(iterate.astype(jnp.bfloat16), iterate, shift)
        iterate = iterate + relax * (source - image)
    adjoint = iterate.astype(jnp.bfloat16)
    partial_density = jnp.sum(orbitals.astype(jnp.float32) * iterate, axis=1)
    restrict_full = restrict.astype(jnp.float32)
    density_term = lax.psum(partial_density, "orb")
    projected = jnp.dot(density_term, restrict_full, precision=lax.Precision.HIGHEST)
    coarse_cols = projected.shape[1]
    dest_owner = owner[:, 0]
    owner_hot = (dest_owner[:, None] == jnp.arange(n_domains, dtype=jnp.int32)[None, :]).astype(
        jnp.int32
    )
    earlier = jnp.cumsum(owner_hot, axis=0) - owner_hot
    rank_within = jnp.sum(earlier * owner_hot, axis=1)
    slot_index = dest_owner * capacity + rank_within
    send_hot_int = (
        slot_index[None, :] == jnp.arange(n_domains * capacity, dtype=jnp.int32)[:, None]
    ).astype(jnp.int32)
    send_hot = send_hot_int.astype(jnp.float32)
    send_values = jnp.dot(send_hot, projected, precision=lax.Precision.HIGHEST).reshape(
        n_domains, capacity, coarse_cols
    )
    send_ids = (jnp.sum(send_hot_int * (pot_slot + 1)[None, :], axis=1) - 1).reshape(
        n_domains, capacity
    )
    recv_values, recv_ids = (
        lax.all_to_all(send_values, "dom", split_axis=0, concat_axis=0, tiled=True),
        lax.all_to_all(send_ids, "dom", split_axis=0, concat_axis=0, tiled=True),
    )
    recv_hot = (
        recv_ids.reshape(-1)[None, :] == jnp.arange(pot_rows, dtype=jnp.int32)[:, None]
    ).astype(jnp.float32)
    summed = jnp.dot(
        recv_hot, recv_values.reshape(-1, coarse_cols), precision=lax.Precision.HIGHEST
    )
    updated = potential - step_rate * summed
    every_pot = lax.all_gather(updated, "dom", axis=0, tiled=True)
    cell_pot = every_pot[dest_owner * pot_rows + pot_slot]
    node_potential = jnp.dot(cell_pot, prolong.astype(jnp.float32), precision=lax.Precision.HIGHEST)
    shift_new = (base_potential + node_potential)[:, None, :]
    applied = operator(orbitals, orbitals.astype(jnp.float32), shift_new).astype(jnp.bfloat16)
    return (adjoint, updated, applied)


def solution(mesh):
    in_specs = (
        P("dom", "orb", None),
        P("dom", "orb", None),
        P("orb"),
        P("dom"),
        P("dom", None),
        P(),
        P("dom", None),
        P(),
        P(),
        P("dom", None),
        P("dom"),
        P("dom", None),
    )
    out_specs = (P("dom", "orb", None), P("dom", None), P("dom", "orb", None))
    return jax.shard_map(local, mesh=mesh, in_specs=in_specs, out_specs=out_specs, check_vma=False)
```

profile of v0, /device:TPU:2, one launch (start us, length us, event | category | flops | bytes accessed | tf_op | source)
XLA Modules:
  0.0 320.8 jit_solution(6365384118985894531)
XLA Ops:
  7.2 0.0 all-reduce.2.cloned.1.call-start
  7.3 1.0 copy-done
  8.2 1.6 fusion.10
  9.8 11.4 %collective-permute-start.1 = (f32[1,8,64]{2,1,0:T(8,128)S(1)}, f32[1,8,64]{2,1,0:T(8,128)S(1)}, u32[]{:S(2)}, u32[]{:S(2)}) collective-permute-start(f32[1,8,64]{2,1,0:T(8,128)S(1)} %slice.159), channel_id=1, source_target_pairs={{8,0},{16,8},{24,16},{32,24},{40,32},{48,40},{56,48},{64,56},{72,6... | collective-permute-start | bytes 6152 | tf_op jit(solution)/shard_map/ppermute | solution.py:19
  21.2 1.4 fusion.9
  22.7 1.9 collective-permute-start
  24.6 0.1 fusion.77
  24.7 0.1 reduce_window_sum.11
  24.7 0.2 select_reduce_fusion.1
  24.9 0.1 select_reduce_fusion
  25.1 0.2 slice.157
  25.4 1.4 fusion.15
  26.8 3.5 %collective-permute-done = f32[1,8,64]{2,1,0:T(8,128)S(1)} collective-permute-done((f32[1,8,64]{2,1,0:T(8,128)S(1)}, f32[1,8,64]{2,1,0:T(8,128)S(1)}, u32[]{:S(2)}, u32[]{:S(2)}) %collective-permute-start) | collective-permute-done | bytes 2080 | tf_op jit(solution)/shard_map/ppermute | solution.py:16
  30.3 0.8 fusion.11
  31.2 2.6 collective-permute-start.3
  33.8 1.4 fusion.7
  35.3 0.2 slice.164
  35.5 3.3 %collective-permute-start.2 = (f32[1,8,64]{2,1,0:T(8,128)S(1)}, f32[1,8,64]{2,1,0:T(8,128)S(1)}, u32[]{:S(2)}, u32[]{:S(2)}) collective-permute-start(f32[1,8,64]{2,1,0:T(8,128)S(1)} %slice.162), channel_id=1, source_target_pairs={{0,8},{8,16},{16,24},{24,32},{32,40},{40,48},{48,56},{56,64},{64,7... | collective-permute-start | bytes 6152 | tf_op jit(solution)/shard_map/ppermute | solution.py:16
  38.8 1.4 fusion.16
  40.2 2.9 collective-permute-done.2
  43.2 0.6 fusion.27
  43.8 0.4 fusion.12
  44.2 1.9 collective-permute-start.5
  46.1 1.4 fusion.5
  47.6 0.2 slice.171
  47.8 3.9 %collective-permute-start.4 = (f32[1,8,64]{2,1,0:T(8,128)S(1)}, f32[1,8,64]{2,1,0:T(8,128)S(1)}, u32[]{:S(2)}, u32[]{:S(2)}) collective-permute-start(f32[1,8,64]{2,1,0:T(8,128)S(1)} %slice.169), channel_id=1, source_target_pairs={{0,8},{8,16},{16,24},{24,32},{32,40},{40,48},{48,56},{56,64},{64,7... | collective-permute-start | bytes 6152 | tf_op jit(solution)/shard_map/ppermute | solution.py:16
  51.8 1.4 fusion.17
  53.2 2.3 collective-permute-done.4
  55.5 0.8 fusion.13
  56.3 1.9 collective-permute-start.7
  58.3 1.4 fusion.3
  59.8 0.2 slice.178
  60.0 3.9 %collective-permute-start.6 = (f32[1,8,64]{2,1,0:T(8,128)S(1)}, f32[1,8,64]{2,1,0:T(8,128)S(1)}, u32[]{:S(2)}, u32[]{:S(2)}) collective-permute-start(f32[1,8,64]{2,1,0:T(8,128)S(1)} %slice.176), channel_id=1, source_target_pairs={{0,8},{8,16},{16,24},{24,32},{32,40},{40,48},{48,56},{56,64},{64,7... | collective-permute-start | bytes 6152 | tf_op jit(solution)/shard_map/ppermute | solution.py:16
  63.9 1.4 fusion.18
  65.3 2.3 collective-permute-done.6
  67.7 2.1 fusion.24
  69.8 0.0 all-reduce.2.cloned.1.call-update
  69.8 0.8 sub.46
  70.5 5.7 %all-to-all-start = ((s32[64,1,2]{2,1,0:T(1,128)}), s32[64,1,2]{2,1,0:T(1,128)S(1)}, u32[]{:S(2)}, u32[]{:S(2)}) async-start(s32[64,1,2]{2,1,0:T(1,128)} %bitcast.2), calls=%async_computation | async-start | bytes 65536 | tf_op jit(solution)/shard_map/all_to_all | solution.py:103
  76.3 58.1 %all-reduce.2.cloned.1.call-done = f32[48,512]{1,0:T(8,128)} async-done(((f32[48,512]{1,0:T(8,128)}), f32[48,512]{1,0:T(8,128)}) %all-reduce.2.cloned.1.call-update) | async-done | bytes 98320 | tf_op jit(solution)/shard_map/psum | solution.py:81
  134.3 1.1 fusion.90
  135.4 0.3 fusion.74
  135.8 0.7 reshape.85
  136.5 15.9 %all-to-all-start.1 = ((f32[64,1,128]{2,1,0:T(1,128)}), f32[64,1,128]{2,1,0:T(1,128)S(1)}, u32[]{:S(2)}, u32[]{:S(2)}) async-start(f32[64,1,128]{2,1,0:T(1,128)} %reshape.85), calls=%async_computation.1 | async-start | bytes 65536 | tf_op jit(solution)/shard_map/all_to_all | solution.py:102
  152.4 0.0 all-gather.2.cloned.1.call-start
  152.5 0.5 broadcast.70
  153.0 0.7 reduce.3
  153.7 0.1 eq.63
  153.8 12.0 %all-to-all-done.1 = f32[64,1,128]{2,1,0:T(1,128)S(1)} async-done(((f32[64,1,128]{2,1,0:T(1,128)}), f32[64,1,128]{2,1,0:T(1,128)S(1)}, u32[]{:S(2)}, u32[]{:S(2)}) %all-to-all-start.1) | async-done | bytes 32800 | tf_op jit(solution)/shard_map/all_to_all | solution.py:102
  165.9 0.5 broadcast.72
  166.4 0.7 reduce.4
  167.1 0.1 reshape.86
  167.2 0.8 fusion.21
  168.0 128.1 %all-gather.2.cloned.1.call-done = f32[4096,64]{1,0:T(8,128)} async-done(((f32[64,64]{1,0:T(8,128)}), f32[4096,64]{1,0:T(8,128)}) %all-gather.2.cloned.1.call-update) | async-done | bytes 1048592 | tf_op jit(solution)/shard_map/all_gather | solution.py:112
  296.1 2.2 gather_fusion
  298.3 0.2 convolution_add_fusion
  298.5 0.4 fusion.14
  298.9 4.8 %collective-permute-start.9 = (f32[1,8,64]{2,1,0:T(8,128)S(1)}, f32[1,8,64]{2,1,0:T(8,128)S(1)}, u32[]{:S(2)}, u32[]{:S(2)}) collective-permute-start(f32[1,8,64]{2,1,0:T(8,128)S(1)} %slice.187), channel_id=1, source_target_pairs={{8,0},{16,8},{24,16},{32,24},{40,32},{48,40},{56,48},{64,56},{72,6... | collective-permute-start | bytes 6152 | tf_op jit(solution)/shard_map/ppermute | solution.py:19
  303.7 1.4 fusion.1
  305.2 0.1 slice.211
  305.4 1.9 collective-permute-start.8
  307.3 1.6 fusion.20
  308.9 4.1 %collective-permute-done.8 = f32[1,8,64]{2,1,0:T(8,128)S(1)} collective-permute-done((f32[1,8,64]{2,1,0:T(8,128)S(1)}, f32[1,8,64]{2,1,0:T(8,128)S(1)}, u32[]{:S(2)}, u32[]{:S(2)}) %collective-permute-start.8) | collective-permute-done | bytes 2080 | tf_op jit(solution)/shard_map/ppermute | solution.py:16
  313.0 1.0 pad_maximum_fusion
  (58 shorter events, 0.6 us)
Async XLA Ops:
  7.2 1.0 copy-start
  7.2 14.0 %copy-start.11 = (s32[48,64]{1,0:T(8,128)S(1)}, s32[48,64]{1,0:T(8,128)}, u32[]{:S(2)}) copy-start(s32[48,64]{1,0:T(8,128)} %param.18) | copy-start | bytes 36868
  7.2 17.4 %copy-start.7 = (s32[48,1]{0,1:T(1,128)S(1)}, s32[48,1]{0,1:T(1,128)}, u32[]{:S(2)}) copy-start(s32[48,1]{0,1:T(1,128)} %param.21) | copy-start | bytes 580
  7.2 17.7 %copy-start.9 = (s32[48]{0:T(128)S(1)}, s32[48]{0:T(128)}, u32[]{:S(2)}) copy-start(s32[48]{0:T(128)} %param.22) | copy-start | bytes 580
  7.2 127.1 %all-reduce.2.cloned.1.call-start = ((), (), s32[]{:S(2)}) async-start(), calls=%async_computation.2 | async-start | bytes 196608 | tf_op jit(solution)/shard_map/psum | solution.py:81
  9.8 15.5 %collective-permute-start.1 = (f32[1,8,64]{2,1,0:T(8,128)S(1)}, f32[1,8,64]{2,1,0:T(8,128)S(1)}, u32[]{:S(2)}, u32[]{:S(2)}) collective-permute-start(f32[1,8,64]{2,1,0:T(8,128)S(1)} %slice.159), channel_id=1, source_target_pairs={{8,0},{16,8},{24,16},{32,24},{40,32},{48,40},{56,48},{64,56},{72,6... | collective-permute-start | bytes 6152 | tf_op jit(solution)/shard_map/ppermute | solution.py:19
  22.7 7.6 %collective-permute-start = (f32[1,8,64]{2,1,0:T(8,128)S(1)}, f32[1,8,64]{2,1,0:T(8,128)S(1)}, u32[]{:S(2)}, u32[]{:S(2)}) collective-permute-start(f32[1,8,64]{2,1,0:T(8,128)S(1)} %slice.155), channel_id=1, source_target_pairs={{0,8},{8,16},{16,24},{24,32},{32,40},{40,48},{48,56},{56,64},{64,7... | collective-permute-start | bytes 6152 | tf_op jit(solution)/shard_map/ppermute | solution.py:16
  25.0 5.3 %copy-start.1 = (bf16[48,8,512]{2,1,0:T(8,128)(2,1)S(1)}, bf16[48,8,512]{2,1,0:T(8,128)(2,1)}, u32[]{:S(2)}) copy-start(bf16[48,8,512]{2,1,0:T(8,128)(2,1)} %param.13) | copy-start | bytes 1179652
  25.1 5.3 %copy-start.3 = (f32[48,512]{1,0:T(8,128)S(1)}, f32[48,512]{1,0:T(8,128)}, u32[]{:S(2)}) copy-start(f32[48,512]{1,0:T(8,128)} %param.16) | copy-start | bytes 294916
  25.1 5.3 %copy-start.8 = (f32[48]{0:T(128)S(1)}, f32[48]{0:T(128)}, u32[]{:S(2)}) copy-start(f32[48]{0:T(128)} %param.15) | copy-start | bytes 580
  25.1 5.3 %copy-start.10 = (f32[8]{0:T(128)S(1)}, f32[8]{0:T(128)}, u32[]{:S(2)}) copy-start(f32[8]{0:T(128)} %param.14) | copy-start | bytes 100
  31.2 7.6 %collective-permute-start.3 = (f32[1,8,64]{2,1,0:T(8,128)S(1)}, f32[1,8,64]{2,1,0:T(8,128)S(1)}, u32[]{:S(2)}, u32[]{:S(2)}) collective-permute-start(f32[1,8,64]{2,1,0:T(8,128)S(1)} %slice.166), channel_id=1, source_target_pairs={{8,0},{16,8},{24,16},{32,24},{40,32},{48,40},{56,48},{64,56},{72,6... | collective-permute-start | bytes 6152 | tf_op jit(solution)/shard_map/ppermute | solution.py:19
  35.5 7.6 %collective-permute-start.2 = (f32[1,8,64]{2,1,0:T(8,128)S(1)}, f32[1,8,64]{2,1,0:T(8,128)S(1)}, u32[]{:S(2)}, u32[]{:S(2)}) collective-permute-start(f32[1,8,64]{2,1,0:T(8,128)S(1)} %slice.162), channel_id=1, source_target_pairs={{0,8},{8,16},{16,24},{24,32},{32,40},{40,48},{48,56},{56,64},{64,7... | collective-permute-start | bytes 6152 | tf_op jit(solution)/shard_map/ppermute | solution.py:16
  44.2 7.6 %collective-permute-start.5 = (f32[1,8,64]{2,1,0:T(8,128)S(1)}, f32[1,8,64]{2,1,0:T(8,128)S(1)}, u32[]{:S(2)}, u32[]{:S(2)}) collective-permute-start(f32[1,8,64]{2,1,0:T(8,128)S(1)} %slice.173), channel_id=1, source_target_pairs={{8,0},{16,8},{24,16},{32,24},{40,32},{48,40},{56,48},{64,56},{72,6... | collective-permute-start | bytes 6152 | tf_op jit(solution)/shard_map/ppermute | solution.py:19
  47.8 7.6 %collective-permute-start.4 = (f32[1,8,64]{2,1,0:T(8,128)S(1)}, f32[1,8,64]{2,1,0:T(8,128)S(1)}, u32[]{:S(2)}, u32[]{:S(2)}) collective-permute-start(f32[1,8,64]{2,1,0:T(8,128)S(1)} %slice.169), channel_id=1, source_target_pairs={{0,8},{8,16},{16,24},{24,32},{32,40},{40,48},{48,56},{56,64},{64,7... | collective-permute-start | bytes 6152 | tf_op jit(solution)/shard_map/ppermute | solution.py:16
  56.3 7.6 %collective-permute-start.7 = (f32[1,8,64]{2,1,0:T(8,128)S(1)}, f32[1,8,64]{2,1,0:T(8,128)S(1)}, u32[]{:S(2)}, u32[]{:S(2)}) collective-permute-start(f32[1,8,64]{2,1,0:T(8,128)S(1)} %slice.180), channel_id=1, source_target_pairs={{8,0},{16,8},{24,16},{32,24},{40,32},{48,40},{56,48},{64,56},{72,6... | collective-permute-start | bytes 6152 | tf_op jit(solution)/shard_map/ppermute | solution.py:19
  59.7 8.0 %copy-start.2 = (bf16[48,8,512]{2,1,0:T(8,128)(2,1)S(1)}, bf16[48,8,512]{2,1,0:T(8,128)(2,1)}, u32[]{:S(2)}) copy-start(bf16[48,8,512]{2,1,0:T(8,128)(2,1)} %param.12) | copy-start | bytes 1179652
  60.0 7.6 %collective-permute-start.6 = (f32[1,8,64]{2,1,0:T(8,128)S(1)}, f32[1,8,64]{2,1,0:T(8,128)S(1)}, u32[]{:S(2)}, u32[]{:S(2)}) collective-permute-start(f32[1,8,64]{2,1,0:T(8,128)S(1)} %slice.176), channel_id=1, source_target_pairs={{0,8},{8,16},{16,24},{24,32},{32,40},{40,48},{48,56},{56,64},{64,7... | collective-permute-start | bytes 6152 | tf_op jit(solution)/shard_map/ppermute | solution.py:16
  67.6 66.7 %copy-start.4 = (bf16[512,64]{0,1:T(8,128)(2,1)S(1)}, bf16[512,64]{0,1:T(8,128)(2,1)}, u32[]{:S(2)}) copy-start(bf16[512,64]{0,1:T(8,128)(2,1)} %param.19) | copy-start | bytes 196612
  67.7 99.5 %copy-start.6 = (f32[64,64]{1,0:T(8,128)S(1)}, f32[64,64]{1,0:T(8,128)}, u32[]{:S(2)}) copy-start(f32[64,64]{1,0:T(8,128)} %param.23) | copy-start | bytes 49156
  67.7 230.6 %copy-start.5 = (bf16[64,512]{1,0:T(8,128)(2,1)S(1)}, bf16[64,512]{1,0:T(8,128)(2,1)}, u32[]{:S(2)}) copy-start(bf16[64,512]{1,0:T(8,128)(2,1)} %param.20) | copy-start | bytes 196612
  70.5 65.9 %all-to-all-start = ((s32[64,1,2]{2,1,0:T(1,128)}), s32[64,1,2]{2,1,0:T(1,128)S(1)}, u32[]{:S(2)}, u32[]{:S(2)}) async-start(s32[64,1,2]{2,1,0:T(1,128)} %bitcast.2), calls=%async_computation | async-start | bytes 65536 | tf_op jit(solution)/shard_map/all_to_all | solution.py:103
  136.5 29.4 %all-to-all-start.1 = ((f32[64,1,128]{2,1,0:T(1,128)}), f32[64,1,128]{2,1,0:T(1,128)S(1)}, u32[]{:S(2)}, u32[]{:S(2)}) async-start(f32[64,1,128]{2,1,0:T(1,128)} %reshape.85), calls=%async_computation.1 | async-start | bytes 65536 | tf_op jit(solution)/shard_map/all_to_all | solution.py:102
  152.4 143.7 %all-gather.2.cloned.1.call-start = ((), (), s32[]{:S(2)}) async-start(), calls=%async_computation.3 | async-start | bytes 2129920 | tf_op jit(solution)/shard_map/all_gather | solution.py:112
  298.9 8.4 %collective-permute-start.9 = (f32[1,8,64]{2,1,0:T(8,128)S(1)}, f32[1,8,64]{2,1,0:T(8,128)S(1)}, u32[]{:S(2)}, u32[]{:S(2)}) collective-permute-start(f32[1,8,64]{2,1,0:T(8,128)S(1)} %slice.187), channel_id=1, source_target_pairs={{8,0},{16,8},{24,16},{32,24},{40,32},{48,40},{56,48},{64,56},{72,6... | collective-permute-start | bytes 6152 | tf_op jit(solution)/shard_map/ppermute | solution.py:19
  305.4 7.6 %collective-permute-start.8 = (f32[1,8,64]{2,1,0:T(8,128)S(1)}, f32[1,8,64]{2,1,0:T(8,128)S(1)}, u32[]{:S(2)}, u32[]{:S(2)}) collective-permute-start(f32[1,8,64]{2,1,0:T(8,128)S(1)} %slice.183), channel_id=1, source_target_pairs={{0,8},{8,16},{16,24},{24,32},{32,40},{40,48},{48,56},{56,64},{64,7... | collective-permute-start | bytes 6152 | tf_op jit(solution)/shard_map/ppermute | solution.py:16
Sparse Core Ops, SparseCore 0:
  69.9 64.3 all-reduce.1
  168.1 127.9 all-gather.1
where the time goes:
time: 321 us
  waiting for transfers between devices  213 us (66%)
  starting transfers between devices  59.2 us (18%)
  matrix products  20.7 us (6%)
  between operations  14.7 us (5%)
  local copies, waits for them, and re-layouts  7.21 us (2%)
  other arithmetic  5.72 us (2%)
    all_gather x1, waiting for transfers between devices, local(): every_pot = lax.all_gather(updated, 'dom', axis=0, tiled=True)  128 us
    psum x1, waiting for transfers between devices, local(): density_term = lax.psum(partial_density, 'orb')  58.1 us
    ppermute x5, starting transfers between devices, padded_2(): lax.ppermute(lax.slice_in_dim(block, 0, width, axis=dim), axis, backward)  22.6 us
    all_to_all x1, starting transfers between devices, local(): lax.all_to_all(send_values, 'dom', split_axis=0, concat_axis=0, tiled=True)  15.9 us
    ppermute x5, waiting for transfers between devices, padded_2(): lax.ppermute(lax.slice_in_dim(block, block.shape[dim] - width, None, axis...  15 us
    ppermute x5, starting transfers between devices, padded_2(): lax.ppermute(lax.slice_in_dim(block, block.shape[dim] - width, None, axis...  15 us
    all_to_all x1, waiting for transfers between devices, local(): lax.all_to_all(send_values, 'dom', split_axis=0, concat_axis=0, tiled=True)  12 us
    dot_general x5, matrix products, assemble_local(): jnp.einsum('ckj,coj->cok', onehot, left_next, precision=lax.Precision.HIG...  7.2 us
  transfers between devices with their start and end apart: 14, of which 8 were waited for; matrix products, arithmetic and copies ran while one was open for 6% of the time, Pallas kernels for 0%

commit v1 on v0

--- a/solution.py
+++ b/solution.py
@@ -78,7 +78,13 @@
     adjoint = iterate.astype(jnp.bfloat16)
     partial_density = jnp.sum(orbitals.astype(jnp.float32) * iterate, axis=1)
     restrict_full = restrict.astype(jnp.float32)
-    density_term = lax.psum(partial_density, "orb")
+    count_2 = lax.axis_size("orb")
+    density_term, far = (partial_density, 1)
+    while far < count_2:
+        density_term = density_term + lax.ppermute(
+            density_term, "orb", [(i_2, i_2 ^ far) for i_2 in range(count_2)]
+        )
+        far = 2 * far
     projected = jnp.dot(density_term, restrict_full, precision=lax.Precision.HIGHEST)
     coarse_cols = projected.shape[1]
     dest_owner = owner[:, 0]

time: 321 us -> 279 us (0.87)
  waiting for transfers between devices: 213 us -> 172 us
    psum x1 -> x0, waiting for transfers between devices: 58.1 us -> none  [local(): density_term = lax.psum(partial_density, 'orb')]
    all_to_all x1, waiting for transfers between devices: 0.01 us -> 12.2 us  [local(): lax.all_to_all(send_ids, 'dom', split_axis=0, concat_axis=0, tiled=True)]
    ppermute x0 -> x3, starting transfers between devices: none -> 10.6 us  [local(): lax.ppermute(density_term, 'orb', [(i_2, i_2 ^ far) for i_2 in range(coun...]
    all_to_all x1, starting transfers between devices: 15.9 us -> 5.66 us  [local(): lax.all_to_all(send_values, 'dom', split_axis=0, concat_axis=0, tiled=True)]
    ppermute x0 -> x3, waiting for transfers between devices: none -> 4.4 us  [local(): lax.ppermute(density_term, 'orb', [(i_2, i_2 ^ far) for i_2 in range(coun...]
  transfers between devices with their start and end apart: 14 -> 16, of which waited for: 8 -> 10; matrix products, arithmetic and copies ran while one was open for 6% -> 7% of each run, Pallas kernels for 0% -> 0%
where the time goes in v1:
time: 279 us
  waiting for transfers between devices  172 us (62%)
  starting transfers between devices  59.6 us (21%)
  matrix products  19.8 us (7%)
  between operations  14.7 us (5%)
  local copies, waits for them, and re-layouts  7.27 us (3%)
  other arithmetic  5.11 us (2%)
    all_gather x1, waiting for transfers between devices, local(): every_pot = lax.all_gather(updated, 'dom', axis=0, tiled=True)  129 us
    ppermute x5, starting transfers between devices, padded_2(): lax.ppermute(lax.slice_in_dim(block, 0, width, axis=dim), axis, backward)  22.5 us
    ppermute x5, starting transfers between devices, padded_2(): lax.ppermute(lax.slice_in_dim(block, block.shape[dim] - width, None, axis...  15.1 us
    ppermute x5, waiting for transfers between devices, padded_2(): lax.ppermute(lax.slice_in_dim(block, block.shape[dim] - width, None, axis...  15 us
    all_to_all x1, waiting for transfers between devices, local(): lax.all_to_all(send_ids, 'dom', split_axis=0, concat_axis=0, tiled=True)  12.2 us
    all_to_all x1, waiting for transfers between devices, local(): lax.all_to_all(send_values, 'dom', split_axis=0, concat_axis=0, tiled=True)  12 us
    ppermute x3, starting transfers between devices, local(): lax.ppermute(density_term, 'orb', [(i_2, i_2 ^ far) for i_2 in range(coun...  10.6 us
    dot_general x5, matrix products, assemble_local(): jnp.einsum('ckj,coj->cok', onehot, left_next, precision=lax.Precision.HIG...  7.2 us
  transfers between devices with their start and end apart: 16, of which 10 were waited for; matrix products, arithmetic and copies ran while one was open for 7% of the time, Pallas kernels for 0%

profile of v1, /device:TPU:2, one launch (start us, length us, event | category | flops | bytes accessed | tf_op | source)
XLA Modules:
  0.0 278.8 jit_solution(17125449044378127406)
XLA Ops:
  7.2 1.0 copy-done
  8.2 1.6 fusion.10
  9.8 11.4 %collective-permute-start.1 = (f32[1,8,64]{2,1,0:T(8,128)S(1)}, f32[1,8,64]{2,1,0:T(8,128)S(1)}, u32[]{:S(2)}, u32[]{:S(2)}) collective-permute-start(f32[1,8,64]{2,1,0:T(8,128)S(1)} %slice.159), channel_id=1, source_target_pairs={{8,0},{16,8},{24,16},{32,24},{40,32},{48,40},{56,48},{64,56},{72,6... | collective-permute-start | bytes 6152 | tf_op jit(solution)/shard_map/ppermute | solution.py:19
  21.2 1.4 fusion.9
  22.7 1.9 collective-permute-start
  24.7 0.2 select_reduce_fusion.1
  25.0 0.2 slice.157
  25.3 1.4 fusion.15
  26.7 3.6 %collective-permute-done = f32[1,8,64]{2,1,0:T(8,128)S(1)} collective-permute-done((f32[1,8,64]{2,1,0:T(8,128)S(1)}, f32[1,8,64]{2,1,0:T(8,128)S(1)}, u32[]{:S(2)}, u32[]{:S(2)}) %collective-permute-start) | collective-permute-done | bytes 2080 | tf_op jit(solution)/shard_map/ppermute | solution.py:16
  30.3 0.8 fusion.11
  31.2 2.4 collective-permute-start.3
  33.7 1.4 fusion.7
  35.2 0.2 slice.164
  35.4 3.4 %collective-permute-start.2 = (f32[1,8,64]{2,1,0:T(8,128)S(1)}, f32[1,8,64]{2,1,0:T(8,128)S(1)}, u32[]{:S(2)}, u32[]{:S(2)}) collective-permute-start(f32[1,8,64]{2,1,0:T(8,128)S(1)} %slice.162), channel_id=1, source_target_pairs={{0,8},{8,16},{16,24},{24,32},{32,40},{40,48},{48,56},{56,64},{64,7... | collective-permute-start | bytes 6152 | tf_op jit(solution)/shard_map/ppermute | solution.py:16
  38.8 1.4 fusion.16
  40.2 2.8 %collective-permute-done.2 = f32[1,8,64]{2,1,0:T(8,128)S(1)} collective-permute-done((f32[1,8,64]{2,1,0:T(8,128)S(1)}, f32[1,8,64]{2,1,0:T(8,128)S(1)}, u32[]{:S(2)}, u32[]{:S(2)}) %collective-permute-start.2) | collective-permute-done | bytes 2080 | tf_op jit(solution)/shard_map/ppermute | solution.py:16
  43.0 0.6 fusion.27
  43.6 0.4 fusion.12
  44.1 1.9 collective-permute-start.5
  46.0 1.4 fusion.5
  47.5 0.2 slice.171
  47.7 3.9 %collective-permute-start.4 = (f32[1,8,64]{2,1,0:T(8,128)S(1)}, f32[1,8,64]{2,1,0:T(8,128)S(1)}, u32[]{:S(2)}, u32[]{:S(2)}) collective-permute-start(f32[1,8,64]{2,1,0:T(8,128)S(1)} %slice.169), channel_id=1, source_target_pairs={{0,8},{8,16},{16,24},{24,32},{32,40},{40,48},{48,56},{56,64},{64,7... | collective-permute-start | bytes 6152 | tf_op jit(solution)/shard_map/ppermute | solution.py:16
  51.7 1.4 fusion.17
  53.1 2.3 collective-permute-done.4
  55.4 0.8 fusion.13
  56.2 1.9 collective-permute-start.7
  58.1 1.4 fusion.3
  59.6 0.2 slice.178
  59.9 3.9 %collective-permute-start.6 = (f32[1,8,64]{2,1,0:T(8,128)S(1)}, f32[1,8,64]{2,1,0:T(8,128)S(1)}, u32[]{:S(2)}, u32[]{:S(2)}) collective-permute-start(f32[1,8,64]{2,1,0:T(8,128)S(1)} %slice.176), channel_id=1, source_target_pairs={{0,8},{8,16},{16,24},{24,32},{32,40},{40,48},{48,56},{56,64},{64,7... | collective-permute-start | bytes 6152 | tf_op jit(solution)/shard_map/ppermute | solution.py:16
  63.8 1.4 fusion.18
  65.2 2.3 collective-permute-done.6
  67.6 1.4 fusion.24
  69.0 2.0 collective-permute-start.8
  71.1 1.2 collective-permute-done.8
  72.3 3.5 %collective-permute-start.9 = (f32[48,512]{1,0:T(8,128)S(1)}, f32[48,512]{1,0:T(8,128)S(1)}, u32[]{:S(2)}, u32[]{:S(2)}) collective-permute-start(f32[48,512]{1,0:T(8,128)S(1)} %add.120), channel_id=1, source_target_pairs={{0,2},{1,3},{2,0},{3,1},{4,6},{5,7},{6,4},{7,5},{8,10},{9,11},{10,... | collective-permute-start | bytes 294920 | tf_op jit(solution)/shard_map/ppermute | solution.py:84
  75.8 0.1 select_reduce_fusion
  75.9 3.2 %collective-permute-done.9 = f32[48,512]{1,0:T(8,128)S(1)} collective-permute-done((f32[48,512]{1,0:T(8,128)S(1)}, f32[48,512]{1,0:T(8,128)S(1)}, u32[]{:S(2)}, u32[]{:S(2)}) %collective-permute-start.9) | collective-permute-done | bytes 98336 | tf_op jit(solution)/shard_map/ppermute | solution.py:84
  79.1 5.1 %collective-permute-start.10 = (f32[48,512]{1,0:T(8,128)S(1)}, f32[48,512]{1,0:T(8,128)S(1)}, u32[]{:S(2)}, u32[]{:S(2)}) collective-permute-start(f32[48,512]{1,0:T(8,128)S(1)} %add.121), channel_id=1, source_target_pairs={{0,4},{1,5},{2,6},{3,7},{4,0},{5,1},{6,2},{7,3},{8,12},{9,13},{10,... | collective-permute-start | bytes 294920 | tf_op jit(solution)/shard_map/ppermute | solution.py:84
  84.2 0.8 sub.46
  85.0 5.7 %all-to-all-start = ((s32[64,1,2]{2,1,0:T(1,128)}), s32[64,1,2]{2,1,0:T(1,128)S(1)}, u32[]{:S(2)}, u32[]{:S(2)}) async-start(s32[64,1,2]{2,1,0:T(1,128)} %bitcast.2), calls=%async_computation | async-start | bytes 65536 | tf_op jit(solution)/shard_map/all_to_all | solution.py:109
  90.7 0.2 fusion.74
  90.9 0.3 fusion.76
  91.2 0.7 reshape.85
  91.9 12.2 %all-to-all-done = s32[64,1,2]{2,1,0:T(1,128)S(1)} async-done(((s32[64,1,2]{2,1,0:T(1,128)}), s32[64,1,2]{2,1,0:T(1,128)S(1)}, u32[]{:S(2)}, u32[]{:S(2)}) %all-to-all-start) | async-done | bytes 544 | tf_op jit(solution)/shard_map/all_to_all | solution.py:109
  104.2 5.7 %all-to-all-start.1 = ((f32[64,1,128]{2,1,0:T(1,128)}), f32[64,1,128]{2,1,0:T(1,128)S(1)}, u32[]{:S(2)}, u32[]{:S(2)}) async-start(f32[64,1,128]{2,1,0:T(1,128)} %reshape.85), calls=%async_computation.1 | async-start | bytes 65536 | tf_op jit(solution)/shard_map/all_to_all | solution.py:108
  109.9 0.5 broadcast.70
  110.4 0.7 reduce.3
  111.1 0.1 eq.63
  111.3 12.0 %all-to-all-done.1 = f32[64,1,128]{2,1,0:T(1,128)S(1)} async-done(((f32[64,1,128]{2,1,0:T(1,128)}), f32[64,1,128]{2,1,0:T(1,128)S(1)}, u32[]{:S(2)}, u32[]{:S(2)}) %all-to-all-start.1) | async-done | bytes 32800 | tf_op jit(solution)/shard_map/all_to_all | solution.py:108
  123.3 0.5 broadcast.72
  123.8 0.7 reduce.4
  124.5 0.1 reshape.86
  124.7 0.8 fusion.21
  125.5 128.6 %all-gather.2.cloned.1.call-done = f32[4096,64]{1,0:T(8,128)} async-done(((f32[64,64]{1,0:T(8,128)}), f32[4096,64]{1,0:T(8,128)}) %all-gather.2.cloned.1.call-update) | async-done | bytes 1048592 | tf_op jit(solution)/shard_map/all_gather | solution.py:118
  254.1 2.2 gather_fusion
  256.2 0.2 convolution_add_fusion
  256.4 0.4 fusion.14
  256.8 4.8 %collective-permute-start.12 = (f32[1,8,64]{2,1,0:T(8,128)S(1)}, f32[1,8,64]{2,1,0:T(8,128)S(1)}, u32[]{:S(2)}, u32[]{:S(2)}) collective-permute-start(f32[1,8,64]{2,1,0:T(8,128)S(1)} %slice.187), channel_id=1, source_target_pairs={{8,0},{16,8},{24,16},{32,24},{40,32},{48,40},{56,48},{64,56},{72,6... | collective-permute-start | bytes 6152 | tf_op jit(solution)/shard_map/ppermute | solution.py:19
  261.6 1.4 fusion.1
  263.1 0.1 slice.211
  263.3 1.9 collective-permute-start.11
  265.2 1.6 fusion.20
  266.8 4.1 %collective-permute-done.11 = f32[1,8,64]{2,1,0:T(8,128)S(1)} collective-permute-done((f32[1,8,64]{2,1,0:T(8,128)S(1)}, f32[1,8,64]{2,1,0:T(8,128)S(1)}, u32[]{:S(2)}, u32[]{:S(2)}) %collective-permute-start.11) | collective-permute-done | bytes 2080 | tf_op jit(solution)/shard_map/ppermute | solution.py:16
  271.0 1.0 pad_maximum_fusion
  (63 shorter events, 0.8 us)
Async XLA Ops:
  7.2 1.0 copy-start
  7.2 14.0 %copy-start.11 = (s32[48,64]{1,0:T(8,128)S(1)}, s32[48,64]{1,0:T(8,128)}, u32[]{:S(2)}) copy-start(s32[48,64]{1,0:T(8,128)} %param.18) | copy-start | bytes 36868
  7.2 17.4 %copy-start.7 = (s32[48,1]{0,1:T(1,128)S(1)}, s32[48,1]{0,1:T(1,128)}, u32[]{:S(2)}) copy-start(s32[48,1]{0,1:T(1,128)} %param.21) | copy-start | bytes 580
  9.8 15.4 %collective-permute-start.1 = (f32[1,8,64]{2,1,0:T(8,128)S(1)}, f32[1,8,64]{2,1,0:T(8,128)S(1)}, u32[]{:S(2)}, u32[]{:S(2)}) collective-permute-start(f32[1,8,64]{2,1,0:T(8,128)S(1)} %slice.159), channel_id=1, source_target_pairs={{8,0},{16,8},{24,16},{32,24},{40,32},{48,40},{56,48},{64,56},{72,6... | collective-permute-start | bytes 6152 | tf_op jit(solution)/shard_map/ppermute | solution.py:19
  22.7 7.6 %collective-permute-start = (f32[1,8,64]{2,1,0:T(8,128)S(1)}, f32[1,8,64]{2,1,0:T(8,128)S(1)}, u32[]{:S(2)}, u32[]{:S(2)}) collective-permute-start(f32[1,8,64]{2,1,0:T(8,128)S(1)} %slice.155), channel_id=1, source_target_pairs={{0,8},{8,16},{16,24},{24,32},{32,40},{40,48},{48,56},{56,64},{64,7... | collective-permute-start | bytes 6152 | tf_op jit(solution)/shard_map/ppermute | solution.py:16
  24.9 5.4 %copy-start.1 = (bf16[48,8,512]{2,1,0:T(8,128)(2,1)S(1)}, bf16[48,8,512]{2,1,0:T(8,128)(2,1)}, u32[]{:S(2)}) copy-start(bf16[48,8,512]{2,1,0:T(8,128)(2,1)} %param.13) | copy-start | bytes 1179652
  24.9 5.4 %copy-start.3 = (f32[48,512]{1,0:T(8,128)S(1)}, f32[48,512]{1,0:T(8,128)}, u32[]{:S(2)}) copy-start(f32[48,512]{1,0:T(8,128)} %param.16) | copy-start | bytes 294916
  24.9 5.4 %copy-start.8 = (f32[48]{0:T(128)S(1)}, f32[48]{0:T(128)}, u32[]{:S(2)}) copy-start(f32[48]{0:T(128)} %param.15) | copy-start | bytes 580
  25.0 5.4 %copy-start.10 = (f32[8]{0:T(128)S(1)}, f32[8]{0:T(128)}, u32[]{:S(2)}) copy-start(f32[8]{0:T(128)} %param.14) | copy-start | bytes 100
  31.2 7.6 %collective-permute-start.3 = (f32[1,8,64]{2,1,0:T(8,128)S(1)}, f32[1,8,64]{2,1,0:T(8,128)S(1)}, u32[]{:S(2)}, u32[]{:S(2)}) collective-permute-start(f32[1,8,64]{2,1,0:T(8,128)S(1)} %slice.166), channel_id=1, source_target_pairs={{8,0},{16,8},{24,16},{32,24},{40,32},{48,40},{56,48},{64,56},{72,6... | collective-permute-start | bytes 6152 | tf_op jit(solution)/shard_map/ppermute | solution.py:19
  35.4 7.6 %collective-permute-start.2 = (f32[1,8,64]{2,1,0:T(8,128)S(1)}, f32[1,8,64]{2,1,0:T(8,128)S(1)}, u32[]{:S(2)}, u32[]{:S(2)}) collective-permute-start(f32[1,8,64]{2,1,0:T(8,128)S(1)} %slice.162), channel_id=1, source_target_pairs={{0,8},{8,16},{16,24},{24,32},{32,40},{40,48},{48,56},{56,64},{64,7... | collective-permute-start | bytes 6152 | tf_op jit(solution)/shard_map/ppermute | solution.py:16
  44.1 7.6 %collective-permute-start.5 = (f32[1,8,64]{2,1,0:T(8,128)S(1)}, f32[1,8,64]{2,1,0:T(8,128)S(1)}, u32[]{:S(2)}, u32[]{:S(2)}) collective-permute-start(f32[1,8,64]{2,1,0:T(8,128)S(1)} %slice.173), channel_id=1, source_target_pairs={{8,0},{16,8},{24,16},{32,24},{40,32},{48,40},{56,48},{64,56},{72,6... | collective-permute-start | bytes 6152 | tf_op jit(solution)/shard_map/ppermute | solution.py:19
  47.7 7.6 %collective-permute-start.4 = (f32[1,8,64]{2,1,0:T(8,128)S(1)}, f32[1,8,64]{2,1,0:T(8,128)S(1)}, u32[]{:S(2)}, u32[]{:S(2)}) collective-permute-start(f32[1,8,64]{2,1,0:T(8,128)S(1)} %slice.169), channel_id=1, source_target_pairs={{0,8},{8,16},{16,24},{24,32},{32,40},{40,48},{48,56},{56,64},{64,7... | collective-permute-start | bytes 6152 | tf_op jit(solution)/shard_map/ppermute | solution.py:16
  56.2 7.6 %collective-permute-start.7 = (f32[1,8,64]{2,1,0:T(8,128)S(1)}, f32[1,8,64]{2,1,0:T(8,128)S(1)}, u32[]{:S(2)}, u32[]{:S(2)}) collective-permute-start(f32[1,8,64]{2,1,0:T(8,128)S(1)} %slice.180), channel_id=1, source_target_pairs={{8,0},{16,8},{24,16},{32,24},{40,32},{48,40},{56,48},{64,56},{72,6... | collective-permute-start | bytes 6152 | tf_op jit(solution)/shard_map/ppermute | solution.py:19
  59.6 8.0 %copy-start.2 = (bf16[48,8,512]{2,1,0:T(8,128)(2,1)S(1)}, bf16[48,8,512]{2,1,0:T(8,128)(2,1)}, u32[]{:S(2)}) copy-start(bf16[48,8,512]{2,1,0:T(8,128)(2,1)} %param.12) | copy-start | bytes 1179652
  59.9 7.6 %collective-permute-start.6 = (f32[1,8,64]{2,1,0:T(8,128)S(1)}, f32[1,8,64]{2,1,0:T(8,128)S(1)}, u32[]{:S(2)}, u32[]{:S(2)}) collective-permute-start(f32[1,8,64]{2,1,0:T(8,128)S(1)} %slice.176), channel_id=1, source_target_pairs={{0,8},{8,16},{16,24},{24,32},{32,40},{40,48},{48,56},{56,64},{64,7... | collective-permute-start | bytes 6152 | tf_op jit(solution)/shard_map/ppermute | solution.py:16
  67.5 3.5 %copy-start.9 = (s32[48]{0:T(128)S(1)}, s32[48]{0:T(128)}, u32[]{:S(2)}) copy-start(s32[48]{0:T(128)} %param.22) | copy-start | bytes 580
  67.5 23.2 %copy-start.4 = (bf16[512,64]{0,1:T(8,128)(2,1)S(1)}, bf16[512,64]{0,1:T(8,128)(2,1)}, u32[]{:S(2)}) copy-start(bf16[512,64]{0,1:T(8,128)(2,1)} %param.19) | copy-start | bytes 196612
  67.5 57.1 %copy-start.6 = (f32[64,64]{1,0:T(8,128)S(1)}, f32[64,64]{1,0:T(8,128)}, u32[]{:S(2)}) copy-start(f32[64,64]{1,0:T(8,128)} %param.23) | copy-start | bytes 49156
  69.0 187.2 %copy-start.5 = (bf16[64,512]{1,0:T(8,128)(2,1)S(1)}, bf16[64,512]{1,0:T(8,128)(2,1)}, u32[]{:S(2)}) copy-start(bf16[64,512]{1,0:T(8,128)(2,1)} %param.20) | copy-start | bytes 196612
  69.0 3.3 %collective-permute-start.8 = (f32[48,512]{1,0:T(8,128)S(1)}, f32[48,512]{1,0:T(8,128)S(1)}, u32[]{:S(2)}, u32[]{:S(2)}) collective-permute-start(f32[48,512]{1,0:T(8,128)S(1)} %get-tuple-element.3), channel_id=1, source_target_pairs={{0,1},{1,0},{2,3},{3,2},{4,5},{5,4},{6,7},{7,6},{8,9},{9,8},{10,11... | collective-permute-start | bytes 294920 | tf_op jit(solution)/shard_map/ppermute | solution.py:84
  72.3 6.7 %collective-permute-start.9 = (f32[48,512]{1,0:T(8,128)S(1)}, f32[48,512]{1,0:T(8,128)S(1)}, u32[]{:S(2)}, u32[]{:S(2)}) collective-permute-start(f32[48,512]{1,0:T(8,128)S(1)} %add.120), channel_id=1, source_target_pairs={{0,2},{1,3},{2,0},{3,1},{4,6},{5,7},{6,4},{7,5},{8,10},{9,11},{10,... | collective-permute-start | bytes 294920 | tf_op jit(solution)/shard_map/ppermute | solution.py:84
  79.1 11.6 %collective-permute-start.10 = (f32[48,512]{1,0:T(8,128)S(1)}, f32[48,512]{1,0:T(8,128)S(1)}, u32[]{:S(2)}, u32[]{:S(2)}) collective-permute-start(f32[48,512]{1,0:T(8,128)S(1)} %add.121), channel_id=1, source_target_pairs={{0,4},{1,5},{2,6},{3,7},{4,0},{5,1},{6,2},{7,3},{8,12},{9,13},{10,... | collective-permute-start | bytes 294920 | tf_op jit(solution)/shard_map/ppermute | solution.py:84
  85.0 19.2 %all-to-all-start = ((s32[64,1,2]{2,1,0:T(1,128)}), s32[64,1,2]{2,1,0:T(1,128)S(1)}, u32[]{:S(2)}, u32[]{:S(2)}) async-start(s32[64,1,2]{2,1,0:T(1,128)} %bitcast.2), calls=%async_computation | async-start | bytes 65536 | tf_op jit(solution)/shard_map/all_to_all | solution.py:109
  104.2 19.1 %all-to-all-start.1 = ((f32[64,1,128]{2,1,0:T(1,128)}), f32[64,1,128]{2,1,0:T(1,128)S(1)}, u32[]{:S(2)}, u32[]{:S(2)}) async-start(f32[64,1,128]{2,1,0:T(1,128)} %reshape.85), calls=%async_computation.1 | async-start | bytes 65536 | tf_op jit(solution)/shard_map/all_to_all | solution.py:108
  109.8 144.2 %all-gather.2.cloned.1.call-start = ((), (), s32[]{:S(2)}) async-start(), calls=%async_computation.2 | async-start | bytes 2129920 | tf_op jit(solution)/shard_map/all_gather | solution.py:118
  256.8 8.4 %collective-permute-start.12 = (f32[1,8,64]{2,1,0:T(8,128)S(1)}, f32[1,8,64]{2,1,0:T(8,128)S(1)}, u32[]{:S(2)}, u32[]{:S(2)}) collective-permute-start(f32[1,8,64]{2,1,0:T(8,128)S(1)} %slice.187), channel_id=1, source_target_pairs={{8,0},{16,8},{24,16},{32,24},{40,32},{48,40},{56,48},{64,56},{72,6... | collective-permute-start | bytes 6152 | tf_op jit(solution)/shard_map/ppermute | solution.py:19
  263.3 7.6 %collective-permute-start.11 = (f32[1,8,64]{2,1,0:T(8,128)S(1)}, f32[1,8,64]{2,1,0:T(8,128)S(1)}, u32[]{:S(2)}, u32[]{:S(2)}) collective-permute-start(f32[1,8,64]{2,1,0:T(8,128)S(1)} %slice.183), channel_id=1, source_target_pairs={{0,8},{8,16},{16,24},{24,32},{32,40},{40,48},{48,56},{56,64},{64,7... | collective-permute-start | bytes 6152 | tf_op jit(solution)/shard_map/ppermute | solution.py:16
Sparse Core Ops, SparseCore 0:
  125.6 128.4 all-gather.1
